TPU v7x, 256 devices: a whole 4x4x8 slice. The times are simulated.
256 devices in a mesh: row: 32 (over z, y_hi, core), col: 8 (over x, y_lo).
Axes of the slice: x: 4, y: 4 (y_hi: 2, y_lo: 2; y = y_hi * 2 + y_lo), z: 8, core: 2. Of those that a mesh axis runs over, the one named last changes fastest.
Arguments:
- covariance: float32 [16384, 16384], P('row', 'col'), may hold values from -6 to 10
- rotations: bfloat16 [2048, 16384], P(None, 'row'), may hold values from -1 to 2
Outputs:
- rotated: bfloat16 [16384, 16384], P('row', 'col')
All inputs are finite; a program needn't handle non-finite values.
Results may differ from a plain program's by a relative error of at most 0.0049.
Values may be sent and summed in bfloat16 or wider, within the bound.
A program may use at most 128 MiB of HBM per device.

v0:
```python
import jax
import jax.numpy as jnp
from jax import lax
from jax.sharding import PartitionSpec as P


def extended(x, sides, width):
    for axis, dim in sides:
        count, length = (lax.axis_size(axis), x.shape[dim])
        up = [(i, (i + 1) % count) for i in range(count - 1)]
        down = [(j, i) for i, j in up]
        last = lax.slice_in_dim(x, length - width, length, axis=dim)
        first = lax.slice_in_dim(x, 0, width, axis=dim)
        before = lax.ppermute(last, axis, up)
        after = lax.ppermute(first, axis, down)
        x = jnp.concatenate([before, x, after], axis=dim)
    return x


def from_root(x, axis, root):
    mine = lax.axis_index(axis) == root
    return lax.psum(jnp.where(mine, x, jnp.zeros_like(x)), axis)


def from_partner(value, axis, bit):
    mask = 2**bit
    pairs = [(source, source ^ mask) for source in range(lax.axis_size(axis))]
    return lax.ppermute(value, axis, pairs)


def shifted(block, axis, distance):
    devices = range(lax.axis_size(axis))
    route = [(i - distance, i) for i in devices if i - distance in devices]
    return lax.ppermute(block, axis, route)


def reorder_columns(matrix, col_index, pairs, tile):
    upper = matrix[:, :tile]
    lower = matrix[:, tile:]
    outgoing = jnp.where(col_index == 0, lower, upper)
    padded = extended(jnp.concatenate([lower, outgoing], axis=1), (("col", 1),), tile)
    from_left = padded[:, :tile]
    from_right = padded[:, padded.shape[1] - tile :]
    new_upper = jnp.where(col_index == 0, upper, from_left)
    new_lower = jnp.where(col_index == pairs - 1, upper, from_right)
    return jnp.concatenate([new_upper, new_lower], axis=1)


def shards(covariance, rotations):
    rows_dev = covariance.shape[0]
    pair = covariance.shape[1]
    group = pair // rows_dev
    tile = pair // 2
    half_group = group // 2
    pairs = lax.axis_size("col")
    bits = group.bit_length() - 1
    row_index = lax.axis_index("row")
    col_index = lax.axis_index("col")
    pieces = []
    for step in range(group):
        got = from_root(rotations, "row", col_index * group + step)
        pieces.append(
            jnp.dot(
                covariance,
                got.astype(jnp.float32),
                precision=lax.Precision.HIGHEST,
                preferred_element_type=jnp.float32,
            )
        )
    turned = jnp.concatenate(pieces, axis=1).astype(jnp.bfloat16)
    strip = turned
    block_cols = rotations
    for bit in range(bits):
        other_strip, other_cols = from_partner((strip, block_cols), "row", bit)
        high = row_index >> bit & 1 == 1
        strip = jnp.where(
            high,
            jnp.concatenate([other_strip, strip], axis=0),
            jnp.concatenate([strip, other_strip], axis=0),
        )
        block_cols = jnp.where(
            high,
            jnp.concatenate([other_cols, block_cols], axis=1),
            jnp.concatenate([block_cols, other_cols], axis=1),
        )
    offset_in_tile = row_index % half_group * rows_dev
    pair_of = row_index // group
    is_upper = row_index // half_group % 2 == 0
    upper_cols = lax.dynamic_slice_in_dim(block_cols, offset_in_tile, rows_dev, 1)
    lower_cols = lax.dynamic_slice_in_dim(block_cols, tile + offset_in_tile, rows_dev, 1)
    both_tiles = lax.dot_general(
        jnp.concatenate([upper_cols, lower_cols], axis=1),
        strip,
        (((0,), (0,)), ((), ())),
        preferred_element_type=jnp.float32,
    ).astype(jnp.bfloat16)
    upper_tile = both_tiles[:rows_dev]
    lower_tile = both_tiles[rows_dev:]
    from_above = shifted(lower_tile, "row", -group)
    sent_rows = jnp.where(
        is_upper,
        jnp.where(pair_of == pairs - 1, upper_tile, from_above),
        jnp.where(pair_of == 0, lower_tile, upper_tile),
    )
    from_below = shifted(sent_rows, "row", half_group)
    half_rows = rows_dev // 2
    mixed_rows = jnp.concatenate([from_above[:half_rows], from_below[half_rows:]], axis=0)
    lower_out = jnp.where(pair_of == pairs - 1, from_below, mixed_rows)
    upper_out = jnp.where(pair_of == 0, upper_tile, from_below)
    result_rows = jnp.where(is_upper, upper_out, lower_out)
    result_rows = reorder_columns(result_rows, col_index, pairs, tile)
    return result_rows


def solution(mesh):
    placed = (P("row", "col"), P(None, "row"))
    return jax.shard_map(
        shards, mesh=mesh, in_specs=placed, out_specs=P("row", "col"), check_vma=False
    )
```

profile of v0, /device:TPU:99, one launch (start us, length us, event | category | flops | bytes accessed | tf_op | source)
XLA Modules:
  0.0 711.8 jit_solution(17796629462000461389)
XLA Ops:
  6.5 0.0 all-reduce.3.cloned.1.call-start
  6.5 5.1 broadcast_select_fusion.3
  11.6 0.0 all-reduce.3.cloned.1.call-update
  11.6 1.6 copy-done
  13.2 2.5 copy.3
  15.7 0.7 collective-permute-start
  16.3 290.2 %all-reduce.3.cloned.1.call-done = (bf16[2048,512]{1,0:T(8,128)(2,1)}, bf16[2048,512]{1,0:T(8,128)(2,1)}, bf16[2048,512]{1,0:T(8,128)(2,1)}, bf16[2048,512]{1,0:T(8,128)(2,1)}) async-done(((bf16[2048,512]{1,0:T(8,128)(2,1)}, bf16[2048,512]{1,0:T(8,128)(2,1)}, bf16[2048,512]{1,0:T(8,128)(2,1)}, bf16[2048,512]{1,0:T(8,128)(2,1)}), (bf16[2048,512]{1,0:T(8,128)(2,1)}, bf16[2048,512]{1,0:T(8,128)(2,1)}, ...) | async-done | bytes 8388624 | tf_op jit(solution)/shard_map/psum | solution.py:22
  306.6 7.2 %fusion.17 = bf16[512,512]{0,1:T(8,128)(2,1)S(1)} fusion(bf16[2048,512]{1,0:T(8,128)(2,1)} %get-tuple-element.5, f32[512,2048]{1,0:T(8,128)} %param.2), kind=kOutput, calls=%fused_computation.31 | convolution fusion | flops 6442713088 | bytes 6815744 | tf_op jit(solution)/shard_map/dot_general | solution.py:63
  313.7 0.0 copy-done.6
  313.7 0.0 copy-done.9
  313.7 0.0 copy-start.8
  313.8 4.2 fusion.16
  318.0 4.7 fusion.15
  322.8 4.2 fusion.14
  327.0 0.0 copy-done.2
  327.0 0.0 copy-start.4
  327.0 0.0 copy-start.1
  327.0 1.5 pad_maximum_fusion
  328.5 0.0 copy-done.4
  328.5 0.0 collective-permute-start.2
  328.5 0.0 collective-permute-done
  328.5 1.0 copy-done.1
  329.5 5.1 maximum_select_fusion.3
  334.6 5.8 collective-permute-start.1
  340.4 0.0 collective-permute-done.2
  340.5 35.6 %maximum_select_fusion.4 = bf16[1024,2048]{0,1:T(8,128)(2,1)} fusion(bf16[512,512]{0,1:T(8,128)(2,1)S(1)} %fusion.17, bf16[512,512]{0,1:T(8,128)(2,1)S(1)} %fusion.16, bf16[512,512]{0,1:T(8,128)(2,1)S(1)} %copy-done.3, bf16[512,512]{0,1:T(8,128)(2,1)S(1)} %copy-done.5, bf16[512,2048]{0,1:T(8,128)(2,1)} %collective-permute-done.2, pred[]{:T(512)S(6)} %eq.43), kind=kLoop, calls=%fused_computation.13 | loop fusion | flops 44040192 | bytes 8388609 | tf_op jit(solution)/shard_map/jit(_where)/select_n | solution.py:76
  376.1 0.2 collective-permute-start.3
  376.3 55.6 %collective-permute-done.1 = bf16[2048,1024]{0,1:T(8,128)(2,1)} collective-permute-done((bf16[2048,1024]{0,1:T(8,128)(2,1)}, bf16[2048,1024]{0,1:T(8,128)(2,1)}, u32[]{:S(2)}, u32[]{:S(2)}) %collective-permute-start.1) | collective-permute-done | bytes 4194336 | tf_op jit(solution)/shard_map/ppermute | solution.py:28
  431.9 7.5 %maximum_select_fusion = bf16[2048,2048]{0,1:T(8,128)(2,1)S(1)} fusion(bf16[2048,1024]{0,1:T(8,128)(2,1)} %maximum_select_fusion.3, bf16[2048,1024]{0,1:T(8,128)(2,1)} %collective-permute-done.1, pred[]{:T(512)S(6)} %eq.42), kind=kLoop, calls=%fused_computation | loop fusion | flops 37748736 | bytes 16777216 | tf_op jit(solution)/shard_map/jit(_where)/select_n | solution.py:81
  439.4 1.8 constant_dynamic-slice_fusion.1
  441.1 80.1 %collective-permute-done.3 = bf16[1024,2048]{0,1:T(8,128)(2,1)} collective-permute-done((bf16[1024,2048]{0,1:T(8,128)(2,1)}, bf16[1024,2048]{0,1:T(8,128)(2,1)}, u32[]{:S(2)}, u32[]{:S(2)}) %collective-permute-start.3) | collective-permute-done | bytes 4194336 | tf_op jit(solution)/shard_map/ppermute | solution.py:28
  521.3 15.9 %fusion.10 = bf16[1024,2048]{1,0:T(8,128)(2,1)} fusion(bf16[1024,2048]{0,1:T(8,128)(2,1)} %maximum_select_fusion.4, bf16[1024,2048]{0,1:T(8,128)(2,1)} %collective-permute-done.3, pred[]{:T(512)S(6)} %eq.42, bf16[2048,512]{0,1:T(8,128)(2,1)} %get-tuple-element.10, bf16[2048,512]{0,1:T(8,128)(2,1)S(1)} %get-tuple-element.9), kind=kOutput, calls=%fused_computation.14 | convolution fusion | flops 8638169088 | bytes 16777216 | tf_op jit(solution)/shard_map/dot_general | solution.py:91
  537.2 3.2 slice.25
  540.4 1.9 collective-permute-start.4
  542.3 48.2 %collective-permute-done.4 = bf16[512,2048]{1,0:T(8,128)(2,1)S(1)} collective-permute-done((bf16[512,2048]{1,0:T(8,128)(2,1)}, bf16[512,2048]{1,0:T(8,128)(2,1)S(1)}, u32[]{:S(2)}, u32[]{:S(2)}) %collective-permute-start.4) | collective-permute-done | bytes 2097184 | tf_op jit(solution)/shard_map/ppermute | solution.py:34
  590.5 3.8 select_select_fusion
  594.3 5.3 collective-permute-start.5
  599.6 0.1 slice.26
  599.7 45.1 %collective-permute-done.5 = bf16[512,2048]{1,0:T(8,128)(2,1)} collective-permute-done((bf16[512,2048]{1,0:T(8,128)(2,1)}, bf16[512,2048]{1,0:T(8,128)(2,1)}, u32[]{:S(2)}, u32[]{:S(2)}) %collective-permute-start.5) | collective-permute-done | bytes 2097184 | tf_op jit(solution)/shard_map/ppermute | solution.py:34
  644.8 1.3 slice.27
  646.1 3.6 fusion.13
  649.7 1.1 broadcast_select_fusion.6
  650.8 1.9 collective-permute-start.6
  652.7 4.3 collective-permute-start.7
  657.0 39.1 %collective-permute-done.6 = bf16[512,1024]{1,0:T(8,128)(2,1)} collective-permute-done((bf16[512,1024]{1,0:T(8,128)(2,1)}, bf16[512,1024]{1,0:T(8,128)(2,1)}, u32[]{:S(2)}, u32[]{:S(2)}) %collective-permute-start.6) | collective-permute-done | bytes 1048608 | tf_op jit(solution)/shard_map/ppermute | solution.py:14
  696.1 5.4 collective-permute-done.7
  701.5 1.7 broadcast_select_fusion.5
  703.2 1.5 pad_maximum_fusion.1
  (11 shorter events, 0.0 us)
Async XLA Ops:
  6.5 300.0 %all-reduce.3.cloned.1.call-start = ((), (), s32[]{:S(2)}) async-start(), calls=%async_computation | async-start | bytes 16777216 | tf_op jit(solution)/shard_map/psum | solution.py:22
  11.6 1.6 copy-start
  15.7 312.8 %collective-permute-start = (bf16[2048,512]{0,1:T(8,128)(2,1)}, bf16[2048,512]{0,1:T(8,128)(2,1)}, u32[]{:S(2)}, u32[]{:S(2)}) collective-permute-start(bf16[2048,512]{0,1:T(8,128)(2,1)} %copy.3), channel_id=1, source_target_pairs={{0,8},{8,0},{16,24},{24,16},{32,40},{40,32},{48,56},{56,48},{64,72... | collective-permute-start | bytes 6291464 | tf_op jit(solution)/shard_map/ppermute | solution.py:28
  306.5 7.2 %copy-start.6 = (f32[512,2048]{1,0:T(8,128)S(1)}, f32[512,2048]{1,0:T(8,128)}, u32[]{:S(2)}) copy-start(f32[512,2048]{1,0:T(8,128)} %param.2) | copy-start | bytes 12582916
  306.6 7.2 %copy-start.9 = (bf16[2048,512]{1,0:T(8,128)(2,1)S(1)}, bf16[2048,512]{1,0:T(8,128)(2,1)}, u32[]{:S(2)}) copy-start(bf16[2048,512]{1,0:T(8,128)(2,1)} %get-tuple-element.6) | copy-start | bytes 6291460
  313.7 4.2 copy-start.8
  318.0 4.7 copy-start.7
  322.7 4.3 copy-start.2
  327.0 1.5 copy-start.4
  327.0 2.5 copy-start.1
  328.5 12.0 %collective-permute-start.2 = (bf16[512,2048]{0,1:T(8,128)(2,1)}, bf16[512,2048]{0,1:T(8,128)(2,1)}, u32[]{:S(2)}, u32[]{:S(2)}) collective-permute-start(bf16[512,2048]{0,1:T(8,128)(2,1)} %pad_maximum_fusion), channel_id=1, source_target_pairs={{0,8},{8,0},{16,24},{24,16},{32,40},{40,32},{48,56},{56,48},{64,72... | collective-permute-start | bytes 6291464 | tf_op jit(solution)/shard_map/ppermute | solution.py:28
  328.5 12.0 %copy-start.3 = (bf16[512,512]{0,1:T(8,128)(2,1)S(1)}, bf16[512,512]{0,1:T(8,128)(2,1)}, u32[]{:S(2)}) copy-start(bf16[512,512]{0,1:T(8,128)(2,1)} %copy-done.2) | copy-start | bytes 1572868
  328.5 12.0 %copy-start.5 = (bf16[512,512]{0,1:T(8,128)(2,1)S(1)}, bf16[512,512]{0,1:T(8,128)(2,1)}, u32[]{:S(2)}) copy-start(bf16[512,512]{0,1:T(8,128)(2,1)} %copy-done.4) | copy-start | bytes 1572868
  334.6 97.3 %collective-permute-start.1 = (bf16[2048,1024]{0,1:T(8,128)(2,1)}, bf16[2048,1024]{0,1:T(8,128)(2,1)}, u32[]{:S(2)}, u32[]{:S(2)}) collective-permute-start(bf16[2048,1024]{0,1:T(8,128)(2,1)} %maximum_select_fusion.3), channel_id=1, source_target_pairs={{0,16},{8,24},{16,0},{24,8},{32,48},{40,56},{48,32},{56,40},{64,80... | collective-permute-start | bytes 12582920 | tf_op jit(solution)/shard_map/ppermute | solution.py:28
  376.1 145.2 %collective-permute-start.3 = (bf16[1024,2048]{0,1:T(8,128)(2,1)}, bf16[1024,2048]{0,1:T(8,128)(2,1)}, u32[]{:S(2)}, u32[]{:S(2)}) collective-permute-start(bf16[1024,2048]{0,1:T(8,128)(2,1)} %maximum_select_fusion.4), channel_id=1, source_target_pairs={{0,16},{8,24},{16,0},{24,8},{32,48},{40,56},{48,32},{56,40},{64,80... | collective-permute-start | bytes 12582920 | tf_op jit(solution)/shard_map/ppermute | solution.py:28
  540.4 50.1 %collective-permute-start.4 = (bf16[512,2048]{1,0:T(8,128)(2,1)}, bf16[512,2048]{1,0:T(8,128)(2,1)S(1)}, u32[]{:S(2)}, u32[]{:S(2)}) collective-permute-start(bf16[512,2048]{1,0:T(8,128)(2,1)} %slice.25), channel_id=1, source_target_pairs={{32,0},{40,8},{48,16},{56,24},{64,32},{72,40},{80,48},{88,56},{96,... | collective-permute-start | bytes 6291464 | tf_op jit(solution)/shard_map/ppermute | solution.py:34
  594.3 50.5 %collective-permute-start.5 = (bf16[512,2048]{1,0:T(8,128)(2,1)}, bf16[512,2048]{1,0:T(8,128)(2,1)}, u32[]{:S(2)}, u32[]{:S(2)}) collective-permute-start(bf16[512,2048]{1,0:T(8,128)(2,1)} %select_select_fusion), channel_id=1, source_target_pairs={{0,16},{8,24},{16,32},{24,40},{32,48},{40,56},{48,64},{56,72},{64,... | collective-permute-start | bytes 6291464 | tf_op jit(solution)/shard_map/ppermute | solution.py:34
  650.8 45.3 %collective-permute-start.6 = (bf16[512,1024]{1,0:T(8,128)(2,1)}, bf16[512,1024]{1,0:T(8,128)(2,1)}, u32[]{:S(2)}, u32[]{:S(2)}) collective-permute-start(bf16[512,1024]{1,0:T(8,128)(2,1)} %get-tuple-element.13), channel_id=1, source_target_pairs={{0,1},{1,2},{2,3},{3,4},{4,5},{5,6},{6,7},{8,9},{9,10},{10,11},{11... | collective-permute-start | bytes 3145736 | tf_op jit(solution)/shard_map/ppermute | solution.py:14
  652.7 48.7 %collective-permute-start.7 = (bf16[512,1024]{1,0:T(8,128)(2,1)S(1)}, bf16[512,1024]{1,0:T(8,128)(2,1)}, u32[]{:S(2)}, u32[]{:S(2)}) collective-permute-start(bf16[512,1024]{1,0:T(8,128)(2,1)S(1)} %get-tuple-element.14), channel_id=1, source_target_pairs={{1,0},{2,1},{3,2},{4,3},{5,4},{6,5},{7,6},{9,8},{10,9},{11,10},{12... | collective-permute-start | bytes 3145736 | tf_op jit(solution)/shard_map/ppermute | solution.py:15
Sparse Core Ops, SparseCore 0:
  11.8 294.7 all-reduce.2
where the time goes:
time: 722 us; the launch traced here: 712 us
  waiting for transfers between devices  564 us (78%)
  other arithmetic  66.5 us (9%)
  matrix products  36.3 us (5%)
  starting transfers between devices  20.1 us (3%)
  between operations  13.8 us (2%)
  local copies, waits for them, and re-layouts  11.4 us (2%)
    psum x1, waiting for transfers between devices, from_root(): return lax.psum(jnp.where(mine, x, jnp.zeros_like(x)), axis)  290 us
    ppermute x4, waiting for transfers between devices, from_partner(): return lax.ppermute(value, axis, pairs)  136 us
    ppermute x2, waiting for transfers between devices, shifted(): return lax.ppermute(block, axis, route)  93.3 us
    ppermute x1, waiting for transfers between devices, extended(): before = lax.ppermute(last, axis, up)  39.1 us
    select_n x1, other arithmetic, shards(): jnp.where(high, jnp.concatenate([other_strip, strip], axis=0), jnp.concat...  35.6 us
    dot_general x4, matrix products, shards(): jnp.dot(covariance, got.astype(jnp.float32), precision=lax.Precision.HIGH...  20.3 us
    dot_general x1, matrix products, shards(): lax.dot_general(jnp.concatenate([upper_cols, lower_cols], axis=1), strip,...  15.9 us
  transfers between devices with their start and end apart: 9, of which 7 were waited for; matrix products, arithmetic and copies ran while one was open for 10% of the time, Pallas kernels for 0%

commit v1 on v0

v1 whole, which is shorter than its diff:
```python
import functools

import jax
import jax.numpy as jnp
from jax import lax
from jax.experimental import pallas as pl
from jax.experimental.pallas import tpu as pltpu
from jax.sharding import PartitionSpec as P

MESH = pl.DeviceIdType.MESH
PLANES = 8
COLUMNS = 8
XS = 4
BF16 = jnp.bfloat16


def row_of(z, hi, k):
    return z * 4 + hi * 2 + k


def kernel(
    c_ref,
    m_ref,
    o_ref,
    c_raw,
    m_raw,
    c_all,
    m_t,
    m_q,
    t_out,
    t_in,
    y_out,
    c_load,
    m_load,
    c_send,
    c_recv,
    p_send,
    p_recv,
    v_send,
    v_recv,
    x_send,
    x_recv,
    s_send,
    s_recv,
    g_send,
    g_recv,
    t_send,
    t_recv,
    y_send,
    y_recv,
):
    rows, pair = c_ref.shape
    width = m_ref.shape[1]
    piece = width // 4
    half = pair // 2
    small = piece // 2
    tile = pair // 2

    r = lax.axis_index("row")
    c = lax.axis_index("col")
    z, hi, k = r // 4, r // 2 % 2, r % 2
    x, lo = c // 2, c % 2

    mate = (row_of(z, hi, 1 - k), c)
    z_next = (row_of((z + 1) % PLANES, hi, k), c)
    z_prev = (row_of((z + PLANES - 1) % PLANES, hi, k), c)
    across = (row_of(z, 1 - hi, k), x * 2 + 1 - lo)
    x_next = (r, (x + 1) % XS * 2 + lo)
    x_prev = (r, (x + XS - 1) % XS * 2 + lo)

    out_piece = x // 2 * 4 + hi * 2 + x % 2
    out_hi = jnp.where(lo == z % 2, hi, 1 - hi)
    scatter_to = (row_of(out_piece, out_hi, k), z)
    scatter_self = (out_piece == z) & (out_hi == hi) & (z == c)
    in_hi = z // 2 % 2
    in_x = z // 4 * 2 + z % 2
    in_lo = jnp.where(hi == in_hi, c % 2, 1 - c % 2)
    scatter_from = (row_of(c, in_hi, k), in_x * 2 + in_lo)

    t_col = (
        jnp.where(c == 0, 0, jnp.where(c == COLUMNS - 1, c, c + 1)),
        jnp.where(c == 0, 1, c - 1),
    )
    t_slot = (jnp.where(c == COLUMNS - 1, 1, 0), jnp.where(c == 0, 0, 1))
    src_col = jnp.where(
        hi == 0,
        jnp.where(c <= 1, 0, c - 1),
        jnp.where(c == COLUMNS - 1, c, c + 1),
    )
    src_tile = jnp.where(
        hi == 0, jnp.where(c == 1, 1, 0), jnp.where(c == COLUMNS - 1, 0, 1)
    )

    y_z = (
        jnp.where(z == 0, 0, jnp.where(z == PLANES - 1, z, z + 1)),
        jnp.where(z == 0, 1, z - 1),
    )
    y_hi = (jnp.where(z == PLANES - 1, 1, 0), jnp.where(z == 0, 0, 1))
    src_z = jnp.where(
        hi == 0,
        jnp.where(z <= 1, 0, z - 1),
        jnp.where(z == PLANES - 1, z, z + 1),
    )

    barrier = pltpu.get_barrier_semaphore()

    def greet(device):
        pl.semaphore_signal(barrier, inc=1, device_id=device, device_id_type=MESH)

    for device in (mate, z_next, z_prev, across, x_next, x_prev):
        greet(device)
    expected = jnp.int32(6)

    @pl.when(jnp.logical_not(scatter_self))
    def _():
        greet(scatter_from)

    expected = expected + jnp.where(scatter_self, 0, 1)
    for source_hi in range(2):
        device = (row_of(z, source_hi, k), src_col)

        @pl.when((src_col != c) | (hi != source_hi))
        def _():
            greet(device)

    for b in range(2):
        expected = expected + jnp.where((t_col[b] == c) & (t_slot[b] == hi), 0, 1)
    for source_hi in range(2):
        for source_k in range(2):
            device = (row_of(src_z, source_hi, source_k), c)

            @pl.when((src_z != z) | (hi != source_hi) | (k != source_k))
            def _():
                greet(device)

    for b in range(2):
        for h in range(2):
            stays = (y_z[b] == z) & (y_hi[b] == hi) & (k == h)
            expected = expected + jnp.where(stays, 0, 1)

    def remote(src, dst, send, recv, device):
        return pltpu.make_async_remote_copy(
            src_ref=src,
            dst_ref=dst,
            send_sem=send,
            recv_sem=recv,
            device_id=device,
            device_id_type=MESH,
        )

    c_step = rows // 4

    def c_copy(i):
        at = pl.ds(i * c_step, c_step)
        return pltpu.make_async_copy(c_ref.at[at], c_raw.at[at], c_load.at[i])

    m_copy = pltpu.make_async_copy(m_ref, m_raw, m_load)
    m_copy.start()
    for i in range(4):
        c_copy(i).start()

    pl.semaphore_wait(barrier, expected)

    def scatter(h):
        at = pl.ds(h * half, half)
        src = m_ref.at[at, pl.ds(pl.multiple_of(x * piece, piece), piece)]
        return remote(
            src, m_q.at[out_piece, at], s_send.at[h], s_recv.at[h], scatter_to
        )

    def scatter_local(h):
        at = pl.ds(h * half, half)
        src = m_ref.at[at, pl.ds(pl.multiple_of(x * piece, piece), piece)]
        return pltpu.make_async_copy(src, m_q.at[z, at], s_recv.at[h])

    def scatter_in(h):
        at = pl.ds(h * half, half)
        ref = m_q.at[z, at]
        return remote(ref, ref, s_send.at[h], s_recv.at[h], mate)

    @pl.when(scatter_self)
    def _():
        for h in range(2):
            scatter_local(h).start()

    @pl.when(jnp.logical_not(scatter_self))
    def _():
        for h in range(2):
            scatter(h).start()

    m_copy.wait()
    shard = hi * 2 + k
    other = (1 - hi) * 2 + k
    mate_other = (1 - hi) * 2 + 1 - k

    def t_rows(which, quarter, count=piece, start=0):
        at = pl.multiple_of(which * width + quarter * piece + start, small)
        return m_t.at[pl.ds(at, count)]

    def turn(quarter):
        cols = pl.ds(pl.multiple_of(quarter * piece, piece), piece)
        to = pl.ds(pl.multiple_of(shard * width + quarter * piece, piece), piece)
        m_t[to, :] = m_raw[:, cols].T

    to_across = remote(
        t_rows(shard, x), t_rows(shard, x), v_send, v_recv, across
    )
    from_across = remote(
        t_rows(other, x), t_rows(other, x), v_send, v_recv, across
    )
    turn(x)
    to_across.start()

    def c_rows(core, i):
        at = pl.multiple_of(core * rows + i * c_step, c_step)
        return c_all.at[pl.ds(at, c_step)]

    def c_out(i):
        return remote(c_rows(k, i), c_rows(k, i), c_send.at[i], c_recv.at[i], mate)

    def c_in(i):
        ref = c_rows(1 - k, i)
        return remote(ref, ref, c_send.at[i], c_recv.at[i], mate)

    for i in range(4):
        c_copy(i).wait()
        at = pl.multiple_of(k * rows + i * c_step, c_step)
        c_all[pl.ds(at, c_step), :] = c_raw[pl.ds(i * c_step, c_step), :].astype(BF16)
        c_out(i).start()

    for step in range(1, 4):
        turn((x + step) % XS)
    own = pl.ds(pl.multiple_of(shard * width, width), width)
    shard_out = remote(m_t.at[own], m_t.at[own], p_send.at[0], p_recv.at[0], mate)
    shard_out.start()
    mates = pl.ds(
        pl.multiple_of((hi * 2 + 1 - k) * width, width), width
    )
    shard_in = remote(m_t.at[mates], m_t.at[mates], p_send.at[0], p_recv.at[0], mate)

    def relay(i, quarter):
        ref = t_rows(other, quarter)
        return remote(ref, ref, p_send.at[i], p_recv.at[i], mate)

    def relay_in(i, quarter):
        ref = t_rows(mate_other, quarter)
        return remote(ref, ref, p_send.at[i], p_recv.at[i], mate)

    def x_near(way, quarter):
        ref = t_rows(other, quarter)
        device = (x_next, x_prev)[way]
        return remote(ref, ref, x_send.at[way, 0], x_recv.at[way, 0], device)

    def x_far(way, quarter):
        ref = t_rows(other, quarter, small, way * small)
        device = (x_next, x_prev)[way]
        return remote(ref, ref, x_send.at[way, 1], x_recv.at[way, 1], device)

    x_behind = ((x + XS - 1) % XS, (x + 1) % XS)
    x_two = (x + 2) % XS

    def ring(way, distance, h):
        j = ((z + PLANES - distance) % PLANES, (z + distance) % PLANES)[way]
        ref = m_q.at[j, pl.ds(h * half, half)]
        device = (z_next, z_prev)[way]
        at = (way, distance, h)
        return remote(ref, ref, g_send.at[at], g_recv.at[at], device)

    def ring_in(way, distance, h):
        j = ((z + PLANES - distance) % PLANES, (z + distance) % PLANES)[way]
        ref = m_q.at[j, pl.ds(h * half, half)]
        at = (way, distance - 1, h)
        return remote(ref, ref, g_send.at[at], g_recv.at[at], z_next)

    def tile_of(j):
        return j // 2 % 2, j // 4 * 2 + j % 2

    def first(pieces, slot):
        step = min(256, 2 * rows)
        count = len(pieces)

        @pl.loop(0, 2 * rows // step)
        def _(i):
            at = pl.ds(pl.multiple_of(i * step, step), step)
            right = [m_q[j] for j in pieces]
            right = right[0] if count == 1 else jnp.concatenate(right, axis=1)
            got = jnp.dot(c_all[at, :], right, preferred_element_type=jnp.float32)
            got = got.astype(BF16)
            for n in range(count):
                t_out[slot + n, at, :] = got[:, n * piece : (n + 1) * piece]

        for n, j in enumerate(pieces):
            copy, local, away = t_copies(j, slot + n)

            @pl.when(away)
            def _():
                copy.start()

            @pl.when(jnp.logical_not(away))
            def _():
                local.start()

    def t_copies(j, slot):
        b, chunk = tile_of(j)
        col = jnp.where(b == 0, t_col[0], t_col[1])
        to = jnp.where(b == 0, t_slot[0], t_slot[1])
        dst = t_in.at[chunk, pl.ds(pl.multiple_of(hi * tile, tile), tile)]
        recv = t_recv.at[chunk, hi]
        copy = remote(
            t_out.at[slot], dst, t_send.at[slot], recv, (row_of(z, to, k), col)
        )
        local = pltpu.make_async_copy(t_out.at[slot], dst, recv)
        away = (col != c) | (to != hi)
        return copy, local, away

    def y_copies(chunk, b, h):
        g = b * 2 + h
        src = y_out.at[chunk, pl.ds(g * width, width)]
        start = hi * tile + k * width + chunk * piece
        dst = o_ref.at[:, pl.ds(pl.multiple_of(start, piece), piece)]
        recv = y_recv.at[hi, k, chunk]
        device = (row_of(y_z[b], y_hi[b], h), c)
        copy = remote(src, dst, y_send.at[chunk, g], recv, device)
        local = pltpu.make_async_copy(src, dst, recv)
        away = (y_z[b] != z) | (y_hi[b] != hi) | (k != h)
        return copy, local, away

    def second(j):
        tile_index, chunk = tile_of(j)

        @pl.when(tile_index == src_tile)
        def _():
            for source in range(2):
                ref = t_in.at[chunk, pl.ds(source * tile, tile)]
                remote(
                    ref, ref, t_send.at[0], t_recv.at[chunk, source], mate
                ).wait_recv()
            step = min(256, width)
            for b in range(2):
                for h in range(2):
                    base = (b * 2 + h) * width

                    @pl.loop(0, width // step)
                    def _(i):
                        at = pl.ds(pl.multiple_of(base + i * step, step), step)
                        got = jnp.dot(
                            m_t[at, :],
                            t_in[chunk],
                            preferred_element_type=jnp.float32,
                        )
                        y_out[chunk, at, :] = got.astype(BF16)

                    copy, local, away = y_copies(chunk, b, h)

                    @pl.when(away)
                    def _():
                        copy.start()

                    @pl.when(jnp.logical_not(away))
                    def _():
                        local.start()

    for h in range(2):
        scatter_in(h).wait_recv()
        for way in range(2):
            ring(way, 0, h).start()
    for i in range(4):
        c_in(i).wait_recv()
    first([z], 0)
    from_across.wait_recv()
    for way in range(2):
        x_near(way, x).start()
    relay(1, x).start()

    for distance in range(1, 4):
        for h in range(2):
            for way in range(2):
                ring_in(way, distance, h).wait_recv()
                if distance < 3 or h == way:
                    ring(way, distance, h).start()
        ahead, behind = (z + distance) % PLANES, (z + PLANES - distance) % PLANES
        first([behind, ahead], 2 * distance - 1)
        if distance == 1:
            for way in range(2):
                x_near(way, x_behind[way]).wait_recv()
                x_far(way, x_behind[way]).start()
                relay(2 + way, x_behind[way]).start()
        if distance == 2:
            for way in range(2):
                x_far(way, x_two).wait_recv()
            relay(4, x_two).start()
            shard_in.wait_recv()
            for i, quarter in enumerate((x, x_behind[0], x_behind[1], x_two)):
                relay_in(1 + i, quarter).wait_recv()
            second(z)
        if distance >= 2:
            second((z + PLANES - distance + 1) % PLANES)
            second((z + distance - 1) % PLANES)
    for way in range(2):
        ring_in(way, 4, way).wait_recv()
    first([(z + 4) % PLANES], 7)
    second((z + PLANES - 3) % PLANES)
    second((z + 3) % PLANES)
    second((z + 4) % PLANES)

    @pl.when(jnp.logical_not(scatter_self))
    def _():
        for h in range(2):
            scatter(h).wait_send()

    to_across.wait_send()
    shard_out.wait_send()
    for i in range(4):
        c_out(i).wait_send()
    for i, quarter in enumerate((x, x_behind[0], x_behind[1], x_two)):
        relay(1 + i, quarter).wait_send()
    for way in range(2):
        x_near(way, x).wait_send()
        x_far(way, x_behind[way]).wait_send()
        for distance in range(4):
            for h in range(2):
                if distance < 3 or h == way:
                    ring(way, distance, h).wait_send()
    order = [z]
    for distance in range(1, 4):
        order += [(z + PLANES - distance) % PLANES, (z + distance) % PLANES]
    order += [(z + 4) % PLANES]
    for slot, j in enumerate(order):
        copy, local, away = t_copies(j, slot)

        @pl.when(away)
        def _():
            copy.wait_send()

    for chunk in range(4):
        for b in range(2):
            for h in range(2):
                copy, local, away = y_copies(chunk, b, h)

                @pl.when(away)
                def _():
                    copy.wait_send()

    for source_hi in range(2):
        for source_k in range(2):
            for chunk in range(4):
                start = source_hi * tile + source_k * width + chunk * piece
                ref = o_ref.at[:, pl.ds(start, piece)]
                remote(
                    ref, ref, t_send.at[0], y_recv.at[source_hi, source_k, chunk], mate
                ).wait_recv()


def shards(covariance, rotations):
    rows, pair = covariance.shape
    width = rotations.shape[1]
    piece = width // 4
    dma = pltpu.SemaphoreType.DMA
    return pl.pallas_call(
        kernel,
        out_shape=jax.ShapeDtypeStruct((rows, pair), BF16),
        in_specs=[pl.BlockSpec(memory_space=pl.ANY)] * 2,
        out_specs=pl.BlockSpec(memory_space=pl.ANY),
        scratch_shapes=[
            pltpu.VMEM((rows, pair), jnp.float32),
            pltpu.VMEM((pair, width), BF16),
            pltpu.VMEM((2 * rows, pair), BF16),
            pltpu.VMEM((pair, pair), BF16),
            pltpu.VMEM((PLANES, pair, piece), BF16),
            pltpu.VMEM((PLANES, 2 * rows, piece), BF16),
            pltpu.VMEM((4, pair, piece), BF16),
            pltpu.VMEM((4, pair, piece), BF16),
            dma((4,)),
            dma,
            dma((4,)),
            dma((4,)),
            dma((5,)),
            dma((5,)),
            dma,
            dma,
            dma((2, 2)),
            dma((2, 2)),
            dma((2,)),
            dma((2,)),
            dma((2, 4, 2)),
            dma((2, 4, 2)),
            dma((PLANES,)),
            dma((4, 2)),
            dma((4, 4)),
            dma((2, 2, 4)),
        ],
        compiler_params=pltpu.CompilerParams(
            collective_id=0,
            has_side_effects=True,
            vmem_limit_bytes=56 * 1024 * 1024,
        ),
        cost_estimate=pl.CostEstimate(
            flops=4 * rows * pair * pair, bytes_accessed=8 * rows * pair, transcendentals=0
        ),
    )(covariance, rotations)


def solution(mesh):
    placed = (P("row", "col"), P(None, "row"))
    return jax.shard_map(
        shards, mesh=mesh, in_specs=placed, out_specs=P("row", "col"), check_vma=False
    )
```

time: 722 us -> 159 us (0.22)
  the two profiles are of different devices: /device:TPU:99 before, /device:TPU:231 now
where the time goes in v1:
time: 159 us
  Pallas kernels  156 us (98%)
  local copies, waits for them, and re-layouts  3.16 us (2%)
    pallas_call x1, Pallas kernels, shards(): pl.pallas_call(kernel, out_shape=jax.ShapeDtypeStruct((rows, pair), BF16)...  156 us

profile of v1, /device:TPU:231, one launch (start us, length us, event | category | flops | bytes accessed | tf_op | source)
XLA Modules:
  0.0 159.3 jit_solution(15360995269133217148)
XLA Ops:
  0.0 156.1 %shard_map.28 = bf16[512,2048]{1,0:T(8,128)(2,1)} custom-call(f32[512,2048]{1,0:T(8,128)} %c_ref.1, bf16[2048,512]{1,0:T(8,128)(2,1)} %m_ref.1), custom_call_target="tpu_custom_call" | custom-call | flops 8589934592 | bytes 8388608 | tf_op jit(solution)/shard_map/pallas_call | solution.py:459
  156.2 3.2 %copy.4 = bf16[512,2048]{1,0:T(8,128)(2,1)} copy(bf16[512,2048]{1,0:T(8,128)(2,1)} %shard_map.28) | data formatting | bytes 4194304

commit v2 on v0

v2 whole, which is shorter than its diff:
```python
import functools

import jax
import jax.numpy as jnp
from jax import lax
from jax.experimental import pallas as pl
from jax.experimental.pallas import tpu as pltpu
from jax.sharding import PartitionSpec as P

MESH = pl.DeviceIdType.MESH
PLANES = 8
COLUMNS = 8
XS = 4
BF16 = jnp.bfloat16


def row_of(z, hi, k):
    return z * 4 + hi * 2 + k


CHUNKS = 16
SLACK = 2
C_CHUNKS = 8


def kernel(
    c_ref,
    m_ref,
    o_ref,
    c_raw,
    m_raw,
    c_all,
    m_t,
    m_q,
    turned_in,
    t_all,
    y_out,
    c_load,
    m_load,
    q_load,
    c_send,
    c_recv,
    e_send,
    e_recv,
    f_send,
    f_recv,
    p_send,
    p_recv,
    v_send,
    v_recv,
    x_send,
    x_recv,
    r_send,
    r_recv,
    g_send,
    g_recv,
    y_send,
    y_recv,
):
    rows, pair = c_ref.shape
    width = m_ref.shape[1]
    piece = width // 4
    half = pair // 2
    tile = pair // 2

    r = lax.axis_index("row")
    c = lax.axis_index("col")
    z, hi, k = r // 4, r // 2 % 2, r % 2
    x, lo = c // 2, c % 2

    mate = (row_of(z, hi, 1 - k), c)
    twin = (row_of(z, 1 - hi, k), c)
    z_next = (row_of((z + 1) % PLANES, hi, k), c)
    z_prev = (row_of((z + PLANES - 1) % PLANES, hi, k), c)
    across = (row_of(z, 1 - hi, k), x * 2 + 1 - lo)
    x_others = [(r, (x + n) % XS * 2 + lo) for n in range(1, XS)]

    last = COLUMNS - 1
    to_col = jnp.where(
        hi == 0,
        jnp.where(c == 0, 0, jnp.where(c == last, c, c + 1)),
        jnp.where(c == 0, 1, c - 1),
    )
    to_slot = jnp.where(hi == 0, jnp.where(c == last, 1, 0), jnp.where(c == 0, 0, 1))
    src_col = (jnp.where(c <= 1, 0, c - 1), jnp.where(c == last, c, c + 1))
    src_tile = (jnp.where(c == 1, 1, 0), jnp.where(c == last, 0, 1))

    y_z = (
        jnp.where(z == 0, 0, jnp.where(z == PLANES - 1, z, z + 1)),
        jnp.where(z == 0, 1, z - 1),
    )
    y_hi = (jnp.where(z == PLANES - 1, 1, 0), jnp.where(z == 0, 0, 1))
    src_z = jnp.where(
        hi == 0,
        jnp.where(z <= 1, 0, z - 1),
        jnp.where(z == PLANES - 1, z, z + 1),
    )

    barrier = pltpu.get_barrier_semaphore()

    def greet(device):
        pl.semaphore_signal(barrier, inc=1, device_id=device, device_id_type=MESH)

    for device in (mate, twin, z_next, z_prev, across, *x_others):
        greet(device)
    expected = jnp.int32(8)
    for slot in range(2):
        for h in range(2):
            same = (src_z == z) & (src_tile[slot] == hi) & (h == k)
            same = same & (src_col[slot] == c)
            device = (row_of(src_z, src_tile[slot], h), src_col[slot])

            @pl.when(jnp.logical_not(same))
            def _():
                greet(device)

    def stays(b, h):
        return (y_z[b] == z) & (y_hi[b] == hi) & (h == k) & (to_col == c)

    for b in range(2):
        for h in range(2):
            expected = expected + jnp.where(stays(b, h), 0, 1)

    def remote(src, dst, send, recv, device):
        return pltpu.make_async_remote_copy(
            src_ref=src,
            dst_ref=dst,
            send_sem=send,
            recv_sem=recv,
            device_id=device,
            device_id_type=MESH,
        )

    c_step = rows // C_CHUNKS

    def c_copy(i):
        at = pl.ds(i * c_step, c_step)
        return pltpu.make_async_copy(c_ref.at[at], c_raw.at[at], c_load.at[i])

    up = (z - c + PLANES) % PLANES
    down = (c - z + PLANES) % PLANES
    m_copy = pltpu.make_async_copy(m_ref, m_raw, m_load)
    q_copy = pltpu.make_async_copy(m_ref, m_q, q_load)

    @pl.when(up == 0)
    def _():
        q_copy.start()

    for i in range(C_CHUNKS):
        c_copy(i).start()
    m_copy.start()

    pl.semaphore_wait(barrier, expected)

    def over(part):
        at = pl.ds(part * half, half)
        src = m_ref.at[at, pl.ds(pl.multiple_of(x * piece, piece), piece)]
        return remote(
            src, turned_in.at[at], v_send.at[part], v_recv.at[part], across
        )

    for part in range(2):
        over(part).start()

    def c_rows(of_hi, core, i):
        at = pl.multiple_of(of_hi * tile + core * rows + i * c_step, c_step)
        return c_all.at[pl.ds(at, c_step)]

    def c_mate(i):
        ref = c_rows(hi, k, i)
        return remote(ref, ref, c_send.at[i], c_recv.at[i], mate)

    def c_mate_in(i):
        ref = c_rows(hi, 1 - k, i)
        return remote(ref, ref, c_send.at[i], c_recv.at[i], mate)

    def c_twin(i):
        ref = c_rows(hi, k, i)
        return remote(ref, ref, e_send.at[i], e_recv.at[i], twin)

    def c_twin_in(i):
        ref = c_rows(1 - hi, k, i)
        return remote(ref, ref, e_send.at[i], e_recv.at[i], twin)

    def c_relay(i):
        ref = c_rows(1 - hi, k, i)
        return remote(ref, ref, f_send.at[i], f_recv.at[i], mate)

    def c_relay_in(i):
        ref = c_rows(1 - hi, 1 - k, i)
        return remote(ref, ref, f_send.at[i], f_recv.at[i], mate)

    for part in range(2):
        over(part).wait_recv()
    for i in range(C_CHUNKS):
        c_copy(i).wait()
        at = pl.multiple_of(hi * tile + k * rows + i * c_step, c_step)
        c_all[pl.ds(at, c_step), :] = c_raw[pl.ds(i * c_step, c_step), :].astype(BF16)
        c_twin(i).start()

    @pl.when(up == 0)
    def _():
        q_copy.wait()

    q_step = half // CHUNKS

    def spread(way, n):
        at = pl.multiple_of(way * half + n * q_step, q_step)
        ref = m_q.at[pl.ds(at, q_step)]
        device = (z_next, z_prev)[way]
        return remote(ref, ref, g_send.at[way, n], g_recv.at[way, n], device)

    def pass_on(s):
        for way, distance in ((0, up), (1, down)):
            n = s - SLACK * distance
            here = (n >= 0) & (n < CHUNKS)

            @pl.when(here & (distance > 0))
            def _():
                spread(way, n).wait_recv()

            @pl.when(here & (distance < PLANES - 1))
            def _():
                spread(way, n).start()

    every = 4

    def slots(first, end):
        @pl.loop(first, end)
        def _(s):
            pass_on(s)

            @pl.when((s % every == every - 1) & (s < every * C_CHUNKS))
            def _():
                i = s // every
                c_twin_in(i).wait_recv()
                c_relay(i).start()

    slots(0, 2)

    m_copy.wait()
    shard = hi * 2 + k
    other = (1 - hi) * 2 + k
    mate_other = (1 - hi) * 2 + 1 - k

    def t_rows(which, quarter):
        return pl.ds(pl.multiple_of(which * width + quarter * piece, piece), piece)

    for i in range(C_CHUNKS):
        c_mate(i).start()
    for quarter in range(4):
        m_t[t_rows(shard, quarter), :] = m_raw[
            :, quarter * piece : (quarter + 1) * piece
        ].T
    own = pl.ds(pl.multiple_of(shard * width, width), width)
    shard_out = remote(m_t.at[own], m_t.at[own], p_send, p_recv, mate)
    shard_out.start()
    mates = pl.ds(pl.multiple_of((hi * 2 + 1 - k) * width, width), width)
    shard_in = remote(m_t.at[mates], m_t.at[mates], p_send, p_recv, mate)

    def along(n, part):
        ref = m_t.at[t_rows(other, x), pl.ds(part * half, half)]
        at = (n - 1, part)
        return remote(ref, ref, x_send.at[at], x_recv.at[at], x_others[n - 1])

    def along_in(n, part):
        quarter = (x + XS - n) % XS
        ref = m_t.at[t_rows(other, quarter), pl.ds(part * half, half)]
        at = (n - 1, part)
        return remote(ref, ref, x_send.at[at], x_recv.at[at], mate)

    def relay(n, part, of=other):
        quarter = (x + XS - n) % XS
        ref = m_t.at[t_rows(of, quarter), pl.ds(part * half, half)]
        return remote(ref, ref, r_send.at[n, part], r_recv.at[n, part], mate)

    def turn_over(part):
        at = slice(part * half, (part + 1) * half)
        m_t[t_rows(other, x), at] = turned_in[at, :].T
        for n in range(1, XS):
            along(n, part).start()
        relay(0, part).start()

    slots(2, 14)
    turn_over(0)
    slots(14, 24)
    turn_over(1)
    slots(24, CHUNKS + SLACK * (PLANES - 1))

    def first(start, count):
        step = min(256, count)

        @pl.loop(0, count // step)
        def _(i):
            at = pl.ds(pl.multiple_of(start + i * step, step), step)
            got = jnp.dot(c_all[at, :], m_q[...], preferred_element_type=jnp.float32)
            t_all[at, :] = got.astype(BF16)

    for i in range(C_CHUNKS):
        c_mate_in(i).wait_recv()
    first(hi * tile, tile)
    left = (CHUNKS + SLACK * (PLANES - 1)) // every
    for i in range(left, C_CHUNKS):
        c_twin_in(i).wait_recv()
        c_relay(i).start()
    first((1 - hi) * tile + k * rows, rows)
    for i in range(C_CHUNKS):
        c_relay_in(i).wait_recv()
    first((1 - hi) * tile + (1 - k) * rows, rows)
    for part in range(2):
        for n in range(1, XS):
            along_in(n, part).wait_recv()
            relay(n, part).start()
    shard_in.wait_recv()
    for part in range(2):
        for n in range(XS):
            relay(n, part, mate_other).wait_recv()

    def y_copies(b, h):
        src = y_out.at[pl.ds((b * 2 + h) * width, width)]
        place = to_slot * tile + k * width
        dst = o_ref.at[:, pl.ds(pl.multiple_of(place, width), width)]
        recv = y_recv.at[to_slot, k]
        device = (row_of(y_z[b], y_hi[b], h), to_col)
        copy = remote(src, dst, y_send.at[b, h], recv, device)
        return copy, pltpu.make_async_copy(src, dst, recv)

    for b in range(2):
        for h in range(2):
            base = (b * 2 + h) * width
            step = min(256, width)

            @pl.loop(0, width // step)
            def _(i):
                at = pl.ds(pl.multiple_of(base + i * step, step), step)
                got = jnp.dot(m_t[at, :], t_all[...], preferred_element_type=jnp.float32)
                y_out[at, :] = got.astype(BF16)

            copy, local = y_copies(b, h)

            @pl.when(jnp.logical_not(stays(b, h)))
            def _():
                copy.start()

            @pl.when(stays(b, h))
            def _():
                local.start()

    shard_out.wait_send()
    for i in range(C_CHUNKS):
        c_mate(i).wait_send()
        c_twin(i).wait_send()
        c_relay(i).wait_send()
    for part in range(2):
        over(part).wait_send()
        for n in range(XS):
            relay(n, part).wait_send()
        for n in range(1, XS):
            along(n, part).wait_send()

    for way, distance in ((0, up), (1, down)):

        @pl.when(distance < PLANES - 1)
        def _():
            @pl.loop(0, CHUNKS)
            def _(n):
                spread(way, n).wait_send()

    for b in range(2):
        for h in range(2):
            copy, _ = y_copies(b, h)

            @pl.when(jnp.logical_not(stays(b, h)))
            def _():
                copy.wait_send()

    for slot in range(2):
        for h in range(2):
            ref = o_ref.at[:, pl.ds(slot * tile + h * width, width)]
            remote(ref, ref, y_send.at[0, 0], y_recv.at[slot, h], mate).wait_recv()


def shards(covariance, rotations):
    rows, pair = covariance.shape
    width = rotations.shape[1]
    dma = pltpu.SemaphoreType.DMA
    return pl.pallas_call(
        kernel,
        out_shape=jax.ShapeDtypeStruct((rows, pair), BF16),
        in_specs=[pl.BlockSpec(memory_space=pl.ANY)] * 2,
        out_specs=pl.BlockSpec(memory_space=pl.ANY),
        scratch_shapes=[
            pltpu.VMEM((rows, pair), jnp.float32),
            pltpu.VMEM((pair, width), BF16),
            pltpu.VMEM((pair, pair), BF16),
            pltpu.VMEM((pair, pair), BF16),
            pltpu.VMEM((pair, width), BF16),
            pltpu.VMEM((pair, width // 4), BF16),
            pltpu.VMEM((pair, width), BF16),
            pltpu.VMEM((pair, width), BF16),
            dma((C_CHUNKS,)),
            dma,
            dma,
            dma((C_CHUNKS,)),
            dma((C_CHUNKS,)),
            dma((C_CHUNKS,)),
            dma((C_CHUNKS,)),
            dma((C_CHUNKS,)),
            dma((C_CHUNKS,)),
            dma,
            dma,
            dma((2,)),
            dma((2,)),
            dma((XS - 1, 2)),
            dma((XS - 1, 2)),
            dma((XS, 2)),
            dma((XS, 2)),
            dma((2, CHUNKS)),
            dma((2, CHUNKS)),
            dma((2, 2)),
            dma((2, 2)),
        ],
        compiler_params=pltpu.CompilerParams(
            collective_id=0,
            has_side_effects=True,
            vmem_limit_bytes=56 * 1024 * 1024,
        ),
        cost_estimate=pl.CostEstimate(
            flops=4 * rows * pair * pair, bytes_accessed=8 * rows * pair, transcendentals=0
        ),
    )(covariance, rotations)


def solution(mesh):
    placed = (P("row", "col"), P(None, "row"))
    return jax.shard_map(
        shards, mesh=mesh, in_specs=placed, out_specs=P("row", "col"), check_vma=False
    )
```

time: 722 us -> 143 us (0.20)
  the two profiles are of different devices: /device:TPU:99 before, /device:TPU:7 now
where the time goes in v2:
time: 143 us
  Pallas kernels  140 us (98%)
  local copies, waits for them, and re-layouts  3.16 us (2%)
    pallas_call x1, Pallas kernels, shards(): pl.pallas_call(kernel, out_shape=jax.ShapeDtypeStruct((rows, pair), BF16)...  140 us
    unnamed x1, local copies, waits for them, and re-layouts  3.16 us

profile of v2, /device:TPU:7, one launch (start us, length us, event | category | flops | bytes accessed | tf_op | source)
XLA Modules:
  0.0 143.2 jit_solution(17879772987456208789)
XLA Ops:
  0.0 140.1 %shard_map.28 = bf16[512,2048]{1,0:T(8,128)(2,1)} custom-call(f32[512,2048]{1,0:T(8,128)} %c_ref.1, bf16[2048,512]{1,0:T(8,128)(2,1)} %m_ref.1), custom_call_target="tpu_custom_call" | custom-call | flops 8589934592 | bytes 8388608 | tf_op jit(solution)/shard_map/pallas_call | solution.py:387
  140.1 3.2 %copy.4 = bf16[512,2048]{1,0:T(8,128)(2,1)} copy(bf16[512,2048]{1,0:T(8,128)(2,1)} %shard_map.28) | data formatting | bytes 4194304

commit v3 on v2

--- a/solution.py
+++ b/solution.py
@@ -20,6 +20,8 @@
 
 CHUNKS = 16
 SLACK = 2
+HEAD = 6
+EARLY = 6
 C_CHUNKS = 8
 
 
@@ -190,13 +192,11 @@
         ref = c_rows(1 - hi, 1 - k, i)
         return remote(ref, ref, f_send.at[i], f_recv.at[i], mate)
 
-    for part in range(2):
-        over(part).wait_recv()
     for i in range(C_CHUNKS):
         c_copy(i).wait()
         at = pl.multiple_of(hi * tile + k * rows + i * c_step, c_step)
         c_all[pl.ds(at, c_step), :] = c_raw[pl.ds(i * c_step, c_step), :].astype(BF16)
-        c_twin(i).start()
+        c_mate(i).start()
 
     @pl.when(up == 0)
     def _():
@@ -230,13 +230,15 @@
         def _(s):
             pass_on(s)
 
-            @pl.when((s % every == every - 1) & (s < every * C_CHUNKS))
-            def _():
-                i = s // every
+            n = s - HEAD
+
+            @pl.when((n >= 0) & (n % every == every - 1) & (n < every * EARLY))
+            def _():
+                i = n // every
                 c_twin_in(i).wait_recv()
                 c_relay(i).start()
 
-    slots(0, 2)
+    slots(0, HEAD)
 
     m_copy.wait()
     shard = hi * 2 + k
@@ -246,8 +248,6 @@
     def t_rows(which, quarter):
         return pl.ds(pl.multiple_of(which * width + quarter * piece, piece), piece)
 
-    for i in range(C_CHUNKS):
-        c_mate(i).start()
     for quarter in range(4):
         m_t[t_rows(shard, quarter), :] = m_raw[
             :, quarter * piece : (quarter + 1) * piece
@@ -281,11 +281,13 @@
             along(n, part).start()
         relay(0, part).start()
 
-    slots(2, 14)
-    turn_over(0)
-    slots(14, 24)
-    turn_over(1)
-    slots(24, CHUNKS + SLACK * (PLANES - 1))
+    for part in range(2):
+        over(part).wait_recv()
+    for i in range(C_CHUNKS):
+        c_twin(i).start()
+    for part in range(2):
+        turn_over(part)
+    slots(HEAD, CHUNKS + SLACK * (PLANES - 1))
 
     def first(start, count):
         step = min(256, count)
@@ -299,14 +301,18 @@
     for i in range(C_CHUNKS):
         c_mate_in(i).wait_recv()
     first(hi * tile, tile)
-    left = (CHUNKS + SLACK * (PLANES - 1)) // every
-    for i in range(left, C_CHUNKS):
-        c_twin_in(i).wait_recv()
-        c_relay(i).start()
-    first((1 - hi) * tile + k * rows, rows)
-    for i in range(C_CHUNKS):
-        c_relay_in(i).wait_recv()
-    first((1 - hi) * tile + (1 - k) * rows, rows)
+    group = C_CHUNKS // 2
+    part_rows = rows // 2
+    for n in range(2):
+        for i in range(n * group, (n + 1) * group):
+            if i >= EARLY:
+                c_twin_in(i).wait_recv()
+                c_relay(i).start()
+        first((1 - hi) * tile + k * rows + n * part_rows, part_rows)
+    for n in range(2):
+        for i in range(n * group, (n + 1) * group):
+            c_relay_in(i).wait_recv()
+        first((1 - hi) * tile + (1 - k) * rows + n * part_rows, part_rows)
     for part in range(2):
         for n in range(1, XS):
             along_in(n, part).wait_recv()

time: 143 us -> 134 us (0.937)
  Pallas kernels: 140 us -> 131 us
    pallas_call x1, Pallas kernels: 140 us -> 131 us  [shards(): pl.pallas_call(kernel, out_shape=jax.ShapeDtypeStruct((rows, pair), BF16)...]
where the time goes in v3:
time: 134 us
  Pallas kernels  131 us (98%)
  local copies, waits for them, and re-layouts  3.16 us (2%)
    pallas_call x1, Pallas kernels, shards(): pl.pallas_call(kernel, out_shape=jax.ShapeDtypeStruct((rows, pair), BF16)...  131 us
    unnamed x1, local copies, waits for them, and re-layouts  3.16 us

profile of v3, /device:TPU:7, one launch (start us, length us, event | category | flops | bytes accessed | tf_op | source)
XLA Modules:
  0.0 133.9 jit_solution(1260631468300471970)
XLA Ops:
  0.0 130.7 %shard_map.28 = bf16[512,2048]{1,0:T(8,128)(2,1)} custom-call(f32[512,2048]{1,0:T(8,128)} %c_ref.1, bf16[2048,512]{1,0:T(8,128)(2,1)} %m_ref.1), custom_call_target="tpu_custom_call" | custom-call | flops 8589934592 | bytes 8388608 | tf_op jit(solution)/shard_map/pallas_call | solution.py:393
  130.7 3.2 %copy.4 = bf16[512,2048]{1,0:T(8,128)(2,1)} copy(bf16[512,2048]{1,0:T(8,128)(2,1)} %shard_map.28) | data formatting | bytes 4194304

commit v4 on v3

--- a/solution.py
+++ b/solution.py
@@ -20,6 +20,7 @@
 
 CHUNKS = 16
 SLACK = 2
+PARTS = 2
 HEAD = 6
 EARLY = 6
 C_CHUNKS = 8
@@ -37,6 +38,7 @@
     turned_in,
     t_all,
     y_out,
+    hold,
     c_load,
     m_load,
     q_load,
@@ -56,6 +58,9 @@
     r_recv,
     g_send,
     g_recv,
+    h_send,
+    h_recv,
+    w_send,
     y_send,
     y_recv,
 ):
@@ -78,12 +83,17 @@
     x_others = [(r, (x + n) % XS * 2 + lo) for n in range(1, XS)]
 
     last = COLUMNS - 1
-    to_col = jnp.where(
-        hi == 0,
-        jnp.where(c == 0, 0, jnp.where(c == last, c, c + 1)),
-        jnp.where(c == 0, 1, c - 1),
-    )
-    to_slot = jnp.where(hi == 0, jnp.where(c == last, 1, 0), jnp.where(c == 0, 0, 1))
+
+    def column_target(col):
+        to = jnp.where(
+            hi == 0,
+            jnp.where(col == 0, 0, jnp.where(col == last, col, col + 1)),
+            jnp.where(col == 0, 1, col - 1),
+        )
+        upper = jnp.where(col == last, 1, 0)
+        return to, jnp.where(hi == 0, upper, jnp.where(col == 0, 0, 1))
+
+    to_col, to_slot = column_target(c)
     src_col = (jnp.where(c <= 1, 0, c - 1), jnp.where(c == last, c, c + 1))
     src_tile = (jnp.where(c == 1, 1, 0), jnp.where(c == last, 0, 1))
 
@@ -92,11 +102,77 @@
         jnp.where(z == 0, 1, z - 1),
     )
     y_hi = (jnp.where(z == PLANES - 1, 1, 0), jnp.where(z == 0, 0, 1))
-    src_z = jnp.where(
-        hi == 0,
+    src_plane = (
         jnp.where(z <= 1, 0, z - 1),
         jnp.where(z == PLANES - 1, z, z + 1),
     )
+    src_z = jnp.where(hi == 0, src_plane[0], src_plane[1])
+    side_z = jnp.where(hi == 0, src_plane[1], src_plane[0])
+
+    moves_x = to_col // 2 != x
+
+    def own_line(col, h):
+        return (hi == 0) & ((col == last - 1) | ((col == 1) & (h == 1)))
+
+    def side_line(col, col_hi, h):
+        return (h == 1) & (((col == 2) & (col_hi == 1)) | ((col == last) & (col_hi == 0)))
+
+    def route(b, h):
+        own_hi = y_hi[b] == hi
+        line = own_line(c, h)
+        side = side_line(c, hi, h)
+        side_col = jnp.where(c == 2, 3, last - 1)
+        leaves = y_z[b] != z
+        relayed = jnp.where(own_hi, jnp.where(line, leaves, moves_x), leaves)
+        via_hi = jnp.where(own_hi | jnp.logical_not(side), hi, 1 - hi)
+        via_x = jnp.where(line, c, x * 2 + to_col % 2)
+        via_col = jnp.where(own_hi, via_x, jnp.where(side, side_col, c))
+        which = jnp.where(own_hi | side, 1, 0)
+        return relayed, which, (row_of(y_z[b], via_hi, k), via_col)
+
+    def final(b, h):
+        device = (row_of(y_z[b], y_hi[b], h), to_col)
+        return device, (y_z[b] == z) & (y_hi[b] == hi) & (h == k) & (to_col == c)
+
+    peer = x * 2 + 1 - lo
+    peer_col, peer_slot = column_target(peer)
+
+    def relay(n, h):
+        if n == 0:
+            here = (side_z != z) & jnp.logical_not(side_line(c, hi, h))
+            return here, (row_of(side_z, hi, k), c), to_col, to_slot
+        from_peer = (peer_col // 2 != x) & jnp.logical_not(own_line(peer, h))
+        away = src_z != z
+        from_own = away & own_line(c, h)
+        side_col = jnp.where(c == 3, 2, last)
+        from_side = (hi == 0) & (c == 3) | (hi == 1) & (c == last - 1)
+        from_side = away & (h == 1) & from_side
+        source_hi = jnp.where(from_side, 1 - hi, hi)
+        source_col = jnp.where(from_side, side_col, jnp.where(from_own, c, peer))
+        end = jnp.where(c == 3, 1, last)
+        col = jnp.where(from_side, end, jnp.where(from_own, to_col, peer_col))
+        slot = jnp.where(from_side, 1, jnp.where(from_own, to_slot, peer_slot))
+        here = from_peer | from_own | from_side
+        return here, (row_of(src_z, source_hi, k), source_col), col, slot
+
+    relay_hi = (1 - hi, hi)
+
+    def block_from(slot, core):
+        col, source_hi = src_col[slot], src_tile[slot]
+        own_hi = source_hi == hi
+        line = own_line(col, k)
+        side = (source_hi != hi) & side_line(col, source_hi, k)
+        away = src_z != z
+        relayed = jnp.where(own_hi, jnp.where(line, away, col // 2 != x), away)
+        along_x = jnp.where(line, col, col // 2 * 2 + lo)
+        via_col = jnp.where(own_hi, along_x, jnp.where(side, jnp.where(col == 2, 3, last - 1), col))
+        via_hi = jnp.where(side, hi, source_hi)
+        plane = jnp.where(relayed, z, src_z)
+        sender_hi = jnp.where(relayed, via_hi, source_hi)
+        sender_col = jnp.where(relayed, via_col, col)
+        device = (row_of(plane, sender_hi, core), sender_col)
+        same = (plane == z) & (sender_hi == hi) & (core == k) & (sender_col == c)
+        return device, same
 
     barrier = pltpu.get_barrier_semaphore()
 
@@ -106,22 +182,20 @@
     for device in (mate, twin, z_next, z_prev, across, *x_others):
         greet(device)
     expected = jnp.int32(8)
-    for slot in range(2):
+    def greet_if(device, condition):
+        @pl.when(condition)
+        def _():
+            greet(device)
+
+    for n in range(2):
         for h in range(2):
-            same = (src_z == z) & (src_tile[slot] == hi) & (h == k)
-            same = same & (src_col[slot] == c)
-            device = (row_of(src_z, src_tile[slot], h), src_col[slot])
-
-            @pl.when(jnp.logical_not(same))
-            def _():
-                greet(device)
-
-    def stays(b, h):
-        return (y_z[b] == z) & (y_hi[b] == hi) & (h == k) & (to_col == c)
-
-    for b in range(2):
-        for h in range(2):
-            expected = expected + jnp.where(stays(b, h), 0, 1)
+            here, device, _, _ = relay(n, h)
+            greet_if(device, here)
+            expected = expected + jnp.where(here, 1, 0)
+            device, same = block_from(n, h)
+            greet_if(device, jnp.logical_not(same))
+            sends = route(n, h)[0] | jnp.logical_not(final(n, h)[1])
+            expected = expected + jnp.where(sends, 1, 0)
 
     def remote(src, dst, send, recv, device):
         return pltpu.make_async_remote_copy(
@@ -269,7 +343,7 @@
         at = (n - 1, part)
         return remote(ref, ref, x_send.at[at], x_recv.at[at], mate)
 
-    def relay(n, part, of=other):
+    def to_mate(n, part, of=other):
         quarter = (x + XS - n) % XS
         ref = m_t.at[t_rows(of, quarter), pl.ds(part * half, half)]
         return remote(ref, ref, r_send.at[n, part], r_recv.at[n, part], mate)
@@ -279,7 +353,7 @@
         m_t[t_rows(other, x), at] = turned_in[at, :].T
         for n in range(1, XS):
             along(n, part).start()
-        relay(0, part).start()
+        to_mate(0, part).start()
 
     for part in range(2):
         over(part).wait_recv()
@@ -316,41 +390,72 @@
     for part in range(2):
         for n in range(1, XS):
             along_in(n, part).wait_recv()
-            relay(n, part).start()
+            to_mate(n, part).start()
     shard_in.wait_recv()
     for part in range(2):
         for n in range(XS):
-            relay(n, part, mate_other).wait_recv()
-
-    def y_copies(b, h):
-        src = y_out.at[pl.ds((b * 2 + h) * width, width)]
-        place = to_slot * tile + k * width
-        dst = o_ref.at[:, pl.ds(pl.multiple_of(place, width), width)]
-        recv = y_recv.at[to_slot, k]
-        device = (row_of(y_z[b], y_hi[b], h), to_col)
-        copy = remote(src, dst, y_send.at[b, h], recv, device)
-        return copy, pltpu.make_async_copy(src, dst, recv)
-
-    for b in range(2):
-        for h in range(2):
-            base = (b * 2 + h) * width
-            step = min(256, width)
-
-            @pl.loop(0, width // step)
-            def _(i):
-                at = pl.ds(pl.multiple_of(base + i * step, step), step)
+            to_mate(n, part, mate_other).wait_recv()
+
+    part_step = width // PARTS
+
+    def place(slot, core):
+        at = pl.multiple_of(slot * tile + core * width, width)
+        return pl.ds(at, width)
+
+    def y_copies(b, h, part):
+        src = y_out.at[pl.ds((b * 2 + h) * width + part * part_step, part_step)]
+        at = pl.ds(part * part_step, part_step)
+        dst = o_ref.at[at, place(to_slot, k)]
+        recv = y_recv.at[to_slot, k, part]
+        device, same = final(b, h)
+        send = y_send.at[b, h, part]
+        straight = remote(src, dst, send, recv, device)
+        local = pltpu.make_async_copy(src, dst, recv)
+        relayed, n, via = route(b, h)
+        held = hold.at[n, pl.ds(h * width + part * part_step, part_step)]
+        first_hop = remote(src, held, send, h_recv.at[n, h, part], via)
+        return straight, local, first_hop, same, relayed
+
+    def held_in(n, h, part):
+        ref = hold.at[n, pl.ds(h * width + part * part_step, part_step)]
+        return remote(ref, ref, h_send.at[n, h, part], h_recv.at[n, h, part], mate)
+
+    def second_hop(n, h, part):
+        _, _, col, slot = relay(n, h)
+        src = hold.at[n, pl.ds(h * width + part * part_step, part_step)]
+        dst = o_ref.at[pl.ds(part * part_step, part_step), place(slot, k)]
+        device = (row_of(z, relay_hi[n], h), col)
+        recv = y_recv.at[slot, k, part]
+        return remote(src, dst, w_send.at[n, h, part], recv, device)
+
+    for h in range(2):
+        for part in range(PARTS):
+            for b in range(2):
+                at = pl.ds((b * 2 + h) * width + part * part_step, part_step)
                 got = jnp.dot(m_t[at, :], t_all[...], preferred_element_type=jnp.float32)
                 y_out[at, :] = got.astype(BF16)
-
-            copy, local = y_copies(b, h)
-
-            @pl.when(jnp.logical_not(stays(b, h)))
-            def _():
-                copy.start()
-
-            @pl.when(stays(b, h))
-            def _():
-                local.start()
+                straight, local, first_hop, same, relayed = y_copies(b, h, part)
+
+                @pl.when(relayed)
+                def _():
+                    first_hop.start()
+
+                @pl.when(jnp.logical_not(relayed | same))
+                def _():
+                    straight.start()
+
+                @pl.when(jnp.logical_not(relayed) & same)
+                def _():
+                    local.start()
+
+    for h in range(2):
+        for part in range(PARTS):
+            for n in range(2):
+
+                @pl.when(relay(n, h)[0])
+                def _():
+                    held_in(n, h, part).wait_recv()
+                    second_hop(n, h, part).start()
 
     shard_out.wait_send()
     for i in range(C_CHUNKS):
@@ -360,7 +465,7 @@
     for part in range(2):
         over(part).wait_send()
         for n in range(XS):
-            relay(n, part).wait_send()
+            to_mate(n, part).wait_send()
         for n in range(1, XS):
             along(n, part).wait_send()
 
@@ -374,16 +479,28 @@
 
     for b in range(2):
         for h in range(2):
-            copy, _ = y_copies(b, h)
-
-            @pl.when(jnp.logical_not(stays(b, h)))
+            for part in range(PARTS):
+                straight, _, _, same, relayed = y_copies(b, h, part)
+
+                @pl.when(relayed | jnp.logical_not(same))
+                def _():
+                    straight.wait_send()
+
+    for n in range(2):
+        for h in range(2):
+
+            @pl.when(relay(n, h)[0])
             def _():
-                copy.wait_send()
+                for part in range(PARTS):
+                    second_hop(n, h, part).wait_send()
 
     for slot in range(2):
         for h in range(2):
-            ref = o_ref.at[:, pl.ds(slot * tile + h * width, width)]
-            remote(ref, ref, y_send.at[0, 0], y_recv.at[slot, h], mate).wait_recv()
+            for part in range(PARTS):
+                at = pl.ds(part * part_step, part_step)
+                ref = o_ref.at[at, pl.ds(slot * tile + h * width, width)]
+                recv = y_recv.at[slot, h, part]
+                remote(ref, ref, y_send.at[0, 0, 0], recv, mate).wait_recv()
 
 
 def shards(covariance, rotations):
@@ -404,6 +521,7 @@
             pltpu.VMEM((pair, width // 4), BF16),
             pltpu.VMEM((pair, width), BF16),
             pltpu.VMEM((pair, width), BF16),
+            pltpu.VMEM((2, 2 * width, width), BF16),
             dma((C_CHUNKS,)),
             dma,
             dma,
@@ -423,8 +541,11 @@
             dma((XS, 2)),
             dma((2, CHUNKS)),
             dma((2, CHUNKS)),
-            dma((2, 2)),
-            dma((2, 2)),
+            dma((2, 2, PARTS)),
+            dma((2, 2, PARTS)),
+            dma((2, 2, PARTS)),
+            dma((2, 2, PARTS)),
+            dma((2, 2, PARTS)),
         ],
         compiler_params=pltpu.CompilerParams(
             collective_id=0,

time: 134 us -> 125 us (0.933)
  the two profiles are of different devices: /device:TPU:7 before, /device:TPU:9 now
where the time goes in v4:
time: 125 us; the launch traced here: 124 us
  Pallas kernels  121 us (97%)
  local copies, waits for them, and re-layouts  3.16 us (3%)
    pallas_call x1, Pallas kernels, shards(): pl.pallas_call(kernel, out_shape=jax.ShapeDtypeStruct((rows, pair), BF16)...  121 us
    unnamed x1, local copies, waits for them, and re-layouts  3.16 us

profile of v4, /device:TPU:9, one launch (start us, length us, event | category | flops | bytes accessed | tf_op | source)
XLA Modules:
  0.0 124.5 jit_solution(16534397458340549315)
XLA Ops:
  0.0 121.3 %shard_map.28 = bf16[512,2048]{1,0:T(8,128)(2,1)} custom-call(f32[512,2048]{1,0:T(8,128)} %c_ref.1, bf16[2048,512]{1,0:T(8,128)(2,1)} %m_ref.1), custom_call_target="tpu_custom_call" | custom-call | flops 8589934592 | bytes 8388608 | tf_op jit(solution)/shard_map/pallas_call | solution.py:510
  121.3 3.2 %copy.4 = bf16[512,2048]{1,0:T(8,128)(2,1)} copy(bf16[512,2048]{1,0:T(8,128)(2,1)} %shard_map.28) | data formatting | bytes 4194304

commit v5 on v4

--- a/solution.py
+++ b/solution.py
@@ -123,7 +123,7 @@
         side = side_line(c, hi, h)
         side_col = jnp.where(c == 2, 3, last - 1)
         leaves = y_z[b] != z
-        relayed = jnp.where(own_hi, jnp.where(line, leaves, moves_x), leaves)
+        relayed = jnp.where(own_hi, jnp.where(line, leaves, moves_x), leaves | side)
         via_hi = jnp.where(own_hi | jnp.logical_not(side), hi, 1 - hi)
         via_x = jnp.where(line, c, x * 2 + to_col % 2)
         via_col = jnp.where(own_hi, via_x, jnp.where(side, side_col, c))
@@ -146,7 +146,7 @@
         from_own = away & own_line(c, h)
         side_col = jnp.where(c == 3, 2, last)
         from_side = (hi == 0) & (c == 3) | (hi == 1) & (c == last - 1)
-        from_side = away & (h == 1) & from_side
+        from_side = (h == 1) & from_side
         source_hi = jnp.where(from_side, 1 - hi, hi)
         source_col = jnp.where(from_side, side_col, jnp.where(from_own, c, peer))
         end = jnp.where(c == 3, 1, last)
@@ -163,7 +163,7 @@
         line = own_line(col, k)
         side = (source_hi != hi) & side_line(col, source_hi, k)
         away = src_z != z
-        relayed = jnp.where(own_hi, jnp.where(line, away, col // 2 != x), away)
+        relayed = jnp.where(own_hi, jnp.where(line, away, col // 2 != x), away | side)
         along_x = jnp.where(line, col, col // 2 * 2 + lo)
         via_col = jnp.where(own_hi, along_x, jnp.where(side, jnp.where(col == 2, 3, last - 1), col))
         via_hi = jnp.where(side, hi, source_hi)

time: 125 us -> 122 us (0.976)
  Pallas kernels: 121 us -> 119 us
    pallas_call x1, Pallas kernels: 121 us -> 119 us  [shards(): pl.pallas_call(kernel, out_shape=jax.ShapeDtypeStruct((rows, pair), BF16)...]
where the time goes in v5:
time: 122 us
  Pallas kernels  119 us (98%)
  local copies, waits for them, and re-layouts  3.16 us (3%)
    pallas_call x1, Pallas kernels, shards(): pl.pallas_call(kernel, out_shape=jax.ShapeDtypeStruct((rows, pair), BF16)...  119 us
    unnamed x1, local copies, waits for them, and re-layouts  3.16 us

profile of v5, /device:TPU:9, one launch (start us, length us, event | category | flops | bytes accessed | tf_op | source)
XLA Modules:
  0.0 122.2 jit_solution(3705274607061735736)
XLA Ops:
  0.0 119.0 %shard_map.28 = bf16[512,2048]{1,0:T(8,128)(2,1)} custom-call(f32[512,2048]{1,0:T(8,128)} %c_ref.1, bf16[2048,512]{1,0:T(8,128)(2,1)} %m_ref.1), custom_call_target="tpu_custom_call" | custom-call | flops 8589934592 | bytes 8388608 | tf_op jit(solution)/shard_map/pallas_call | solution.py:510
  119.0 3.2 %copy.4 = bf16[512,2048]{1,0:T(8,128)(2,1)} copy(bf16[512,2048]{1,0:T(8,128)(2,1)} %shard_map.28) | data formatting | bytes 4194304

commit v6 on v5

--- a/solution.py
+++ b/solution.py
@@ -18,11 +18,11 @@
     return z * 4 + hi * 2 + k
 
 
-CHUNKS = 16
+CHUNKS = 8
 SLACK = 2
 PARTS = 2
 HEAD = 6
-EARLY = 6
+EARLY = 4
 C_CHUNKS = 8
 
 
@@ -503,11 +503,31 @@
                 remote(ref, ref, y_send.at[0, 0, 0], recv, mate).wait_recv()
 
 
+HAND_ON = 4
+
+
+def hand_on(x_ref, o_ref, held, in_sem, out_sem):
+    step = x_ref.shape[0] // HAND_ON
+
+    def copies(n):
+        at = pl.ds(n * step, step)
+        load = pltpu.make_async_copy(x_ref.at[at], held.at[at], in_sem.at[n])
+        return load, pltpu.make_async_copy(held.at[at], o_ref.at[at], out_sem.at[n])
+
+    for n in range(HAND_ON):
+        copies(n)[0].start()
+    for n in range(HAND_ON):
+        copies(n)[0].wait()
+        copies(n)[1].start()
+    for n in range(HAND_ON):
+        copies(n)[1].wait()
+
+
 def shards(covariance, rotations):
     rows, pair = covariance.shape
     width = rotations.shape[1]
     dma = pltpu.SemaphoreType.DMA
-    return pl.pallas_call(
+    placed = pl.pallas_call(
         kernel,
         out_shape=jax.ShapeDtypeStruct((rows, pair), BF16),
         in_specs=[pl.BlockSpec(memory_space=pl.ANY)] * 2,
@@ -556,6 +576,17 @@
             flops=4 * rows * pair * pair, bytes_accessed=8 * rows * pair, transcendentals=0
         ),
     )(covariance, rotations)
+    return pl.pallas_call(
+        hand_on,
+        out_shape=jax.ShapeDtypeStruct((rows, pair), BF16),
+        in_specs=[pl.BlockSpec(memory_space=pl.ANY)],
+        out_specs=pl.BlockSpec(memory_space=pl.ANY),
+        scratch_shapes=[
+            pltpu.VMEM((rows, pair), BF16),
+            dma((HAND_ON,)),
+            dma((HAND_ON,)),
+        ],
+    )(placed)
 
 
 def solution(mesh):

time: 122 us -> 121 us (level)
  local copies, waits for them, and re-layouts: 3.16 us -> 0 us
  Pallas kernels: 119 us -> 121 us
    unnamed x1 -> x0, local copies, waits for them, and re-layouts: 3.16 us -> none
    pallas_call x0 -> x1, Pallas kernels: none -> 2.42 us  [shards(): pl.pallas_call(hand_on, out_shape=jax.ShapeDtypeStruct((rows, pair), BF16...]
where the time goes in v6:
time: 121 us
  Pallas kernels  121 us (100%)
    pallas_call x1, Pallas kernels, shards(): pl.pallas_call(kernel, out_shape=jax.ShapeDtypeStruct((rows, pair), BF16)...  119 us
    pallas_call x1, Pallas kernels, shards(): pl.pallas_call(hand_on, out_shape=jax.ShapeDtypeStruct((rows, pair), BF16...  2.42 us

profile of v6, /device:TPU:9, one launch (start us, length us, event | category | flops | bytes accessed | tf_op | source)
XLA Modules:
  0.0 121.2 jit_solution(10194079126705117893)
XLA Ops:
  0.0 118.7 %shard_map.28.x_ref = bf16[512,2048]{1,0:T(8,128)(2,1)} custom-call(f32[512,2048]{1,0:T(8,128)} %c_ref.1, bf16[2048,512]{1,0:T(8,128)(2,1)} %m_ref.1), custom_call_target="tpu_custom_call" | custom-call | flops 8589934592 | bytes 8388608 | tf_op jit(solution)/shard_map/pallas_call | solution.py:530
  118.7 2.4 %shard_map.29 = bf16[512,2048]{1,0:T(8,128)(2,1)} custom-call(bf16[512,2048]{1,0:T(8,128)(2,1)} %shard_map.28.x_ref), custom_call_target="tpu_custom_call" | custom-call | tf_op jit(solution)/shard_map/pallas_call | solution.py:579
